TPU v7x, 32 devices: a whole 2x2x4 slice. The times are simulated.
32 devices in a mesh: grp: 4 (over x, core), exp: 8 (over z, y).
Axes of the slice: x: 2, y: 2, z: 4, core: 2. Of those that a mesh axis runs over, the one named last changes fastest.
Arguments:
- tokens: bfloat16 [4096, 4096], P(('grp', 'exp')), may hold values from -6 to 6
- expert_ids: int32 [4096, 8], P(('grp', 'exp')), may hold values from 0 to 15, all different within a row; in each aligned block of 128 rows (0 to 127, 128 to 255, ...) at most 80 rows name the same one
- gate_fixed: int32 [4096, 8], P(('grp', 'exp')), may hold values from 1 to 65535
- w_gate: bfloat16 [16, 4096, 768], P('exp', None, 'grp'), may hold values from -0.09375 to 0.09375
- w_up: bfloat16 [16, 4096, 768], P('exp', None, 'grp'), may hold values from -0.09375 to 0.09375
- w_down: bfloat16 [16, 768, 4096], P('exp', 'grp'), may hold values from -0.21875 to 0.21875
Outputs:
- mixed: bfloat16 [4096, 4096], P(('grp', 'exp'))
Inputs may be any that keep to these rules, and one draw needn't show every extreme that they name: `expert_ids`: each row names 8 different experts. Among the rows of one device no expert is named by more than 80 rows, and in every draw some expert is named by exactly 80 rows of some device.
All inputs are finite; a program needn't handle non-finite values.
Results may differ from a plain program's by a relative error of at most 0.0058.
Values may be sent and summed in bfloat16 or wider, within the bound.
A program may use at most 128 MiB of HBM per device.

v0:
```python
import jax
import jax.numpy as jnp
from jax import lax
from jax.sharding import PartitionSpec as P

EXPERTS = 16
CAP = 80


def expert_apply(rows, gate_panel, up_panel, down_panel):
    gate_part = jnp.dot(rows, gate_panel, preferred_element_type=jnp.float32)
    up_part = jnp.dot(rows, up_panel, preferred_element_type=jnp.float32)
    hidden = (jax.nn.silu(gate_part) * up_part).astype(jnp.bfloat16)
    return jnp.dot(hidden, down_panel, preferred_element_type=jnp.float32).astype(jnp.bfloat16)


def per_device(tokens, expert_ids, gate_fixed, w_gate, w_up, w_down):
    tok_rows, width = tokens.shape
    local_experts = w_gate.shape[0]
    owners = EXPERTS // local_experts
    capacity = CAP
    panels = (
        lax.all_gather(w_gate, "grp", axis=2, tiled=True),
        lax.all_gather(w_up, "grp", axis=2, tiled=True),
        lax.all_gather(w_down, "grp", axis=1, tiled=True),
    )
    gate_full, up_full, down_full = panels
    onehot = (expert_ids[:, :, None] == jnp.arange(EXPERTS, dtype=jnp.int32)[None, None, :]).astype(
        jnp.int32
    )
    routed = jnp.sum(onehot, axis=1)
    slot_te = jnp.cumsum(routed, axis=0) - routed
    slot_tk = jnp.sum(onehot * slot_te[:, None, :], axis=2)
    slot_index = expert_ids * capacity + slot_tk
    owner_cap = min(tok_rows, local_experts * capacity)
    member_tol = routed.reshape(tok_rows, owners, local_experts)
    needs = (jnp.sum(member_tol, axis=2) > 0).astype(jnp.int32)
    owner_slot = jnp.cumsum(needs, axis=0) - needs
    owner_no = jnp.arange(owners, dtype=jnp.int32)
    owner_index = jnp.where(needs > 0, owner_no[None, :] * owner_cap + owner_slot, -1)
    owner_slots = jnp.arange(owners * owner_cap, dtype=jnp.int32)
    owner_select = jnp.sum(
        (owner_index[None, :, :] == owner_slots[:, None, None]).astype(jnp.int32), axis=2
    ).astype(jnp.bfloat16)
    owner_rows = jnp.dot(owner_select, tokens, preferred_element_type=jnp.float32).astype(
        jnp.bfloat16
    )
    owner_rows = owner_rows.reshape(owners, owner_cap, width)
    select_ort = owner_select.reshape(owners, owner_cap, tok_rows).astype(jnp.float32)
    member_sent = jnp.einsum("ort,tol->orl", select_ort, member_tol.astype(jnp.float32)).astype(
        jnp.bfloat16
    )
    came_rows, came_member = (
        lax.all_to_all(owner_rows, "exp", split_axis=0, concat_axis=0, tiled=True),
        lax.all_to_all(member_sent, "exp", split_axis=0, concat_axis=0, tiled=True),
    )
    flat_rows = came_rows.reshape(owners * owner_cap, width)
    extended = jnp.concatenate([flat_rows, jnp.zeros((1, width), flat_rows.dtype)], axis=0)
    source_no = jnp.arange(owners, dtype=jnp.int32)
    per_expert = []
    for local in range(local_experts):
        member = (came_member[:, :, local] > 0).astype(jnp.int32)
        rank = jnp.cumsum(member, axis=1) - member
        target = jnp.where(
            member > 0, source_no[:, None] * capacity + rank, owners * capacity
        ).reshape(owners * owner_cap)
        source_row = jnp.full((owners * capacity,), owners * owner_cap, jnp.int32)
        source_row = source_row.at[target].set(
            jnp.arange(owners * owner_cap, dtype=jnp.int32), mode="drop"
        )
        per_expert.append(extended[source_row].reshape(owners, capacity, width))
    arrived = jnp.stack(per_expert, axis=1)
    outputs = []
    for local in range(local_experts):
        rows = arrived[:, local].reshape(owners * capacity, width)
        done = expert_apply(rows, gate_full[local], up_full[local], down_full[local])
        outputs.append(done.reshape(owners, capacity, width))
    finished = jnp.stack(outputs, axis=1).reshape(EXPERTS, capacity, width)
    returned = lax.all_to_all(finished, "exp", split_axis=0, concat_axis=0, tiled=True)
    gathered = returned.reshape(EXPERTS * capacity, width)[slot_index]
    weight = gate_fixed.astype(jnp.float32) / 65536.0
    mixed = jnp.sum(weight[:, :, None] * gathered.astype(jnp.float32), axis=1)
    return mixed.astype(jnp.bfloat16)


def solution(mesh):
    in_specs = (
        P(("grp", "exp"), None),
        P(("grp", "exp"), None),
        P(("grp", "exp"), None),
        P("exp", None, "grp"),
        P("exp", None, "grp"),
        P("exp", "grp", None),
    )
    out_specs = P(("grp", "exp"), None)
    return jax.shard_map(
        per_device, mesh=mesh, in_specs=in_specs, out_specs=out_specs, check_vma=False
    )
```

profile of v0, /device:TPU:0, one launch (start us, length us, event | category | flops | bytes accessed | tf_op | source)
XLA Modules:
  0.0 581.6 jit_solution(9505664233053339041)
XLA Ops:
  6.5 0.7 all-gather.4.cloned.1.call-update
  7.3 0.7 all-gather.6.cloned.1.call-update
  8.5 1.5 convert_reduce_fusion
  10.0 0.8 convolution_convert_fusion.3
  10.9 7.3 %all-to-all-start.1 = ((bf16[8,128,2]{1,2,0:T(2,128)(2,1)}), bf16[8,128,2]{1,2,0:T(2,128)(2,1)S(1)}, u32[]{:S(2)}, u32[]{:S(2)}) async-start(bf16[8,128,2]{1,2,0:T(2,128)(2,1)} %convolution_convert_fusion.3), calls=%async_computation.1 | async-start | bytes 8192 | tf_op jit(solution)/shard_map/all_to_all | solution.py:55
  18.1 6.9 %convolution_convert_fusion = bf16[1024,4096]{1,0:T(8,128)(2,1)} fusion(bf16[1024,128]{1,0:T(8,128)(2,1)S(1)} %convert_element_type.97, bf16[128,4096]{1,0:T(8,128)(2,1)S(1)} %copy-done), kind=kOutput, calls=%fused_computation.8 | convolution fusion | flops 1077936128 | bytes 9699328 | tf_op jit(solution)/shard_map/dot_general | solution.py:45
  25.0 6.0 %all-to-all-start = ((bf16[8,128,4096]{2,1,0:T(8,128)(2,1)}), bf16[8,128,4096]{2,1,0:T(8,128)(2,1)}, u32[]{:S(2)}, u32[]{:S(2)}) async-start(bf16[8,128,4096]{2,1,0:T(8,128)(2,1)} %bitcast.67), calls=%async_computation | async-start | bytes 16777216 | tf_op jit(solution)/shard_map/all_to_all | solution.py:54
  32.5 4.3 scatter_custom_fusion
  36.8 4.5 scatter_custom_fusion.1
  41.4 172.0 %all-to-all-done = bf16[8,128,4096]{2,1,0:T(8,128)(2,1)} async-done(((bf16[8,128,4096]{2,1,0:T(8,128)(2,1)}), bf16[8,128,4096]{2,1,0:T(8,128)(2,1)}, u32[]{:S(2)}, u32[]{:S(2)}) %all-to-all-start) | async-done | bytes 8388640 | tf_op jit(solution)/shard_map/all_to_all | solution.py:54
  213.4 7.7 %concatenate.3 = bf16[1025,4096]{1,0:T(8,128)(2,1)} pad(bf16[1024,4096]{1,0:T(8,128)(2,1)} %bitcast.2, bf16[]{:T(256)} %constant.16.clone.1), padding=0_1x0_0 | pad | bytes 16785410 | tf_op jit(solution)/shard_map/concatenate | solution.py:58
  221.2 16.1 %gather_fusion = bf16[640,4096]{1,0:T(8,128)(2,1)} fusion(bf16[1025,4096]{1,0:T(8,128)(2,1)} %concatenate.3, s32[1024]{0:T(1024)S(1)} %pad_clamp_fusion.1), kind=kCustom, calls=%fused_computation | custom fusion | bytes 10488320 | tf_op jit(solution)/shard_map/gather | solution.py:71
  237.2 16.5 %gather_fusion.1 = bf16[640,4096]{1,0:T(8,128)(2,1)} fusion(bf16[1025,4096]{1,0:T(8,128)(2,1)} %concatenate.3, s32[1024]{0:T(1024)S(1)} %pad_clamp_fusion), kind=kCustom, calls=%fused_computation.1 | custom fusion | bytes 10488320 | tf_op jit(solution)/shard_map/gather | solution.py:71
  253.8 10.0 %fusion.4 = f32[640,768]{1,0:T(8,128)} fusion(bf16[640,4096]{1,0:T(8,128)(2,1)} %gather_fusion, bf16[2,4096,768]{1,2,0:T(8,128)(2,1)} %all-gather.4.cloned.1.call-done), kind=kOutput, calls=%fused_computation.20 | convolution fusion | flops 4026531840 | bytes 13500416 | tf_op jit(solution)/shard_map/dot_general | solution.py:11
  263.9 4.3 fusion.2
  268.2 9.4 %multiply_convert_fusion.1 = bf16[640,768]{1,0:T(8,128)(2,1)S(1)} fusion(f32[640,768]{1,0:T(8,128)} %fusion.4, bf16[640,4096]{1,0:T(8,128)(2,1)} %gather_fusion, bf16[2,4096,768]{1,2,0:T(8,128)(2,1)} %all-gather.6.cloned.1.call-done), kind=kOutput, calls=%fused_computation.24 | convolution fusion | flops 4029480960 | bytes 14483456 | tf_op jit(solution)/shard_map/dot_general | solution.py:12
  277.6 8.0 %multiply_convert_fusion = bf16[640,768]{1,0:T(8,128)(2,1)} fusion(f32[640,768]{1,0:T(8,128)S(1)} %fusion.2, bf16[640,4096]{1,0:T(8,128)(2,1)} %gather_fusion.1, bf16[2,4096,768]{1,2,0:T(8,128)(2,1)S(1)} %copy-done.6), kind=kOutput, calls=%fused_computation.23 | convolution fusion | flops 4029480960 | bytes 14483456 | tf_op jit(solution)/shard_map/dot_general | solution.py:12
  285.6 9.0 %convolution_convert_fusion.2 = bf16[640,4096]{1,0:T(8,128)(2,1)} fusion(bf16[640,768]{1,0:T(8,128)(2,1)S(1)} %multiply_convert_fusion.1, bf16[2,768,4096]{2,1,0:T(8,128)(2,1)} %all-gather.8.cloned.1.call-done), kind=kOutput, calls=%fused_computation.10 | convolution fusion | flops 4029153280 | bytes 12517376 | tf_op jit(solution)/shard_map/dot_general | solution.py:14
  294.5 5.9 %convolution_convert_fusion.1 = bf16[640,4096]{1,0:T(8,128)(2,1)} fusion(bf16[640,768]{1,0:T(8,128)(2,1)S(1)} %copy-done.8, bf16[2,768,4096]{2,1,0:T(8,128)(2,1)S(1)} %copy-done.7), kind=kOutput, calls=%fused_computation.9 | convolution fusion | flops 4029153280 | bytes 12517376 | tf_op jit(solution)/shard_map/dot_general | solution.py:14
  300.4 9.0 %pad_maximum_fusion = bf16[8,2,80,4096]{3,2,1,0:T(8,128)(2,1)} fusion(bf16[8,1,80,4096]{3,2,1,0:T(8,128)(2,1)} %bitcast.70, bf16[8,1,80,4096]{3,2,1,0:T(8,128)(2,1)} %bitcast.69), kind=kLoop, calls=%fused_computation.7 | loop fusion | flops 5242880 | bytes 20971520 | tf_op jit(solution)/shard_map/stack | solution.py:78
  309.4 5.3 all-to-all-start.2
  315.5 226.0 %all-to-all-done.2 = bf16[16,80,4096]{2,1,0:T(8,128)(2,1)} async-done(((bf16[16,80,4096]{2,1,0:T(8,128)(2,1)}), bf16[16,80,4096]{2,1,0:T(8,128)(2,1)}, u32[]{:S(2)}, u32[]{:S(2)}) %all-to-all-start.2) | async-done | bytes 10485792 | tf_op jit(solution)/shard_map/all_to_all | solution.py:79
  541.5 20.5 %gather_fusion.2 = bf16[1024,4096]{1,0:T(8,128)(2,1)} fusion(bf16[1280,4096]{1,0:T(8,128)(2,1)} %bitcast.24, s32[1024]{0:T(1024)S(1)} %broadcast_clamp_fusion), kind=kCustom, calls=%fused_computation.2 | custom fusion | bytes 16781312 | tf_op jit(solution)/shard_map/gather | solution.py:80
  562.0 12.9 %fusion = bf16[128,4096]{1,0:T(8,128)(2,1)} fusion(bf16[1024,4096]{1,0:T(8,128)(2,1)} %gather_fusion.2, f32[128,8]{1,0:T(8,128)S(1)} %copy.40), kind=kLoop, calls=%fused_computation.6 | loop fusion | flops 12058624 | bytes 9441280 | tf_op jit(solution)/shard_map/reduce_sum | solution.py:82
  (58 shorter events, 2.7 us)
Async XLA Ops:
  6.5 11.6 %copy-start = (bf16[128,4096]{1,0:T(8,128)(2,1)S(1)}, bf16[128,4096]{1,0:T(8,128)(2,1)}, u32[]{:S(2)}) copy-start(bf16[128,4096]{1,0:T(8,128)(2,1)} %param.6) | copy-start | bytes 3145732
  6.5 1.5 copy-start.3
  6.5 247.3 %all-gather.4.cloned.1.call-start = ((), (), s32[]{:S(2)}) async-start(), calls=%async_computation.3 | async-start | bytes 15728640 | tf_op jit(solution)/shard_map/all_gather | solution.py:23
  7.3 260.9 %all-gather.6.cloned.1.call-start = ((), (), s32[]{:S(2)}) async-start(), calls=%async_computation.4 | async-start | bytes 15728640 | tf_op jit(solution)/shard_map/all_gather | solution.py:24
  10.9 14.2 %all-to-all-start.1 = ((bf16[8,128,2]{1,2,0:T(2,128)(2,1)}), bf16[8,128,2]{1,2,0:T(2,128)(2,1)S(1)}, u32[]{:S(2)}, u32[]{:S(2)}) async-start(bf16[8,128,2]{1,2,0:T(2,128)(2,1)} %convolution_convert_fusion.3), calls=%async_computation.1 | async-start | bytes 8192 | tf_op jit(solution)/shard_map/all_to_all | solution.py:55
  25.0 188.4 %all-to-all-start = ((bf16[8,128,4096]{2,1,0:T(8,128)(2,1)}), bf16[8,128,4096]{2,1,0:T(8,128)(2,1)}, u32[]{:S(2)}, u32[]{:S(2)}) async-start(bf16[8,128,4096]{2,1,0:T(8,128)(2,1)} %bitcast.67), calls=%async_computation | async-start | bytes 16777216 | tf_op jit(solution)/shard_map/all_to_all | solution.py:54
  31.1 254.5 %all-gather.8.cloned.1.call-start = ((), (), s32[]{:S(2)}) async-start(), calls=%async_computation.5 | async-start | bytes 15728640 | tf_op jit(solution)/shard_map/all_gather | solution.py:25
  253.8 10.0 %copy-start.2 = (bf16[640,4096]{1,0:T(8,128)(2,1)S(1)}, bf16[640,4096]{1,0:T(8,128)(2,1)}, u32[]{:S(2)}) copy-start(bf16[640,4096]{1,0:T(8,128)(2,1)} %gather_fusion.1) | copy-start | bytes 15728644
  253.8 10.0 %copy-start.5 = (bf16[2,4096,768]{1,2,0:T(8,128)(2,1)S(1)}, bf16[2,4096,768]{1,2,0:T(8,128)(2,1)}, u32[]{:S(2)}) copy-start(bf16[2,4096,768]{1,2,0:T(8,128)(2,1)} %all-gather.4.cloned.1.call-done) | copy-start | bytes 37748740
  268.2 9.4 %copy-start.6 = (bf16[2,4096,768]{1,2,0:T(8,128)(2,1)S(1)}, bf16[2,4096,768]{1,2,0:T(8,128)(2,1)}, u32[]{:S(2)}) copy-start(bf16[2,4096,768]{1,2,0:T(8,128)(2,1)} %all-gather.6.cloned.1.call-done) | copy-start | bytes 37748740
  285.6 9.0 %copy-start.8 = (bf16[640,768]{1,0:T(8,128)(2,1)S(1)}, bf16[640,768]{1,0:T(8,128)(2,1)}, u32[]{:S(2)}) copy-start(bf16[640,768]{1,0:T(8,128)(2,1)} %multiply_convert_fusion) | copy-start | bytes 2949124
  285.6 9.0 %copy-start.7 = (bf16[2,768,4096]{2,1,0:T(8,128)(2,1)S(1)}, bf16[2,768,4096]{2,1,0:T(8,128)(2,1)}, u32[]{:S(2)}) copy-start(bf16[2,768,4096]{2,1,0:T(8,128)(2,1)} %all-gather.8.cloned.1.call-done) | copy-start | bytes 37748740
  309.4 5.9 %copy-start.4 = (s32[128,8]{0,1:T(8,128)S(1)}, s32[128,8]{0,1:T(8,128)}, u32[]{:S(2)}) copy-start(s32[128,8]{0,1:T(8,128)} %param.8) | copy-start | bytes 12292
  309.4 232.1 %all-to-all-start.2 = ((bf16[16,80,4096]{2,1,0:T(8,128)(2,1)}), bf16[16,80,4096]{2,1,0:T(8,128)(2,1)}, u32[]{:S(2)}, u32[]{:S(2)}) async-start(bf16[16,80,4096]{2,1,0:T(8,128)(2,1)} %bitcast.68), calls=%async_computation.2 | async-start | bytes 20971520 | tf_op jit(solution)/shard_map/all_to_all | solution.py:79
  541.5 33.4 %copy-start.1 = (bf16[128,4096]{1,0:T(8,128)(2,1)S(1)}, bf16[128,4096]{1,0:T(8,128)(2,1)}, u32[]{:S(2)}) copy-start(bf16[128,4096]{1,0:T(8,128)(2,1)} %param.6) | copy-start | bytes 3145732
Sparse Core Ops, SparseCore 0:
  8.9 84.7 all-gather.3
  95.3 82.0 all-gather.5
  179.0 82.0 all-gather.7
where the time goes:
time: 588 us; the launch traced here: 582 us
  waiting for transfers between devices  400 us (68%)
  local copies, waits for them, and re-layouts  70.4 us (12%)
  matrix products  54.2 us (9%)
  other arithmetic  24.6 us (4%)
  starting transfers between devices  18.7 us (3%)
  between operations  13.5 us (2%)
    all_to_all x1, waiting for transfers between devices, per_device(): lax.all_to_all(finished, 'exp', split_axis=0, concat_axis=0, tiled=True)  226 us
    all_to_all x1, waiting for transfers between devices, per_device(): lax.all_to_all(owner_rows, 'exp', split_axis=0, concat_axis=0, tiled=True)  172 us
    gather x2, local copies, waits for them, and re-layouts, per_device(): per_expert.append(extended[source_row].reshape(owners, capacity, width))  32.6 us
    gather x1, local copies, waits for them, and re-layouts, per_device(): gathered = returned.reshape(EXPERTS * capacity, width)[slot_index]  20.5 us
    dot_general x2, matrix products, expert_apply(): up_part = jnp.dot(rows, up_panel, preferred_element_type=jnp.float32)  17.3 us
    dot_general x2, matrix products, expert_apply(): jnp.dot(hidden, down_panel, preferred_element_type=jnp.float32)  14.9 us
    dot_general x2, matrix products, expert_apply(): gate_part = jnp.dot(rows, gate_panel, preferred_element_type=jnp.float32)  14.3 us
    reduce_sum x1, other arithmetic, per_device(): mixed = jnp.sum(weight[:, :, None] * gathered.astype(jnp.float32), axis=1)  12.9 us
  transfers between devices with their start and end apart: 6, of which 2 were waited for; matrix products, arithmetic and copies ran while one was open for 16% of the time, Pallas kernels for 0%

commit v1 on v0

v1 whole, which is shorter than its diff:
```python
import jax
import jax.numpy as jnp
from jax import lax
from jax.sharding import Mesh
from jax.sharding import PartitionSpec as P

EXPERTS = 16


def per_device(tokens, expert_ids, gate_fixed, w_gate, w_up, w_down):
    local = w_gate.shape[0]
    onehot = expert_ids[:, :, None] == jnp.arange(EXPERTS, dtype=jnp.int32)[None, None, :]
    weight = jnp.sum(
        jnp.where(onehot, gate_fixed[:, :, None].astype(jnp.float32) / 65536.0, 0.0), axis=1
    )
    all_tokens = lax.all_gather(tokens, ("exp", "x"), axis=0, tiled=True)
    all_weight = lax.all_gather(weight, ("exp", "x"), axis=0, tiled=True)
    gate = lax.all_gather(w_gate, "core", axis=2, tiled=True)
    up = lax.all_gather(w_up, "core", axis=2, tiled=True)
    down = lax.all_gather(w_down, "core", axis=1, tiled=True)
    mine = lax.dynamic_slice_in_dim(all_weight, lax.axis_index("exp") * local, local, axis=1)
    total = None
    for one in range(local):
        gate_part = jnp.dot(all_tokens, gate[one], preferred_element_type=jnp.float32)
        up_part = jnp.dot(all_tokens, up[one], preferred_element_type=jnp.float32)
        hidden = (jax.nn.silu(gate_part) * up_part).astype(jnp.bfloat16)
        done = jnp.dot(hidden, down[one], preferred_element_type=jnp.float32)
        term = mine[:, one : one + 1] * done
        total = term if total is None else total + term
    part = lax.psum_scatter(
        total.astype(jnp.bfloat16), "exp", scatter_dimension=0, tiled=True
    )
    return lax.psum_scatter(part, "x", scatter_dimension=0, tiled=True)


def solution(mesh):
    grp, exp = mesh.shape["grp"], mesh.shape["exp"]
    split = Mesh(mesh.devices.reshape(grp // 2, 2, exp), ("x", "core", "exp"))
    rows = P(("x", "core", "exp"), None)
    in_specs = (
        rows,
        rows,
        rows,
        P("exp", None, ("x", "core")),
        P("exp", None, ("x", "core")),
        P("exp", ("x", "core"), None),
    )
    return jax.shard_map(
        per_device, mesh=split, in_specs=in_specs, out_specs=rows, check_vma=False
    )
```

time: 588 us -> 641 us (1.090)
  waiting for transfers between devices: 400 us -> 488 us
  local copies, waits for them, and re-layouts: 70.4 us -> 0.04 us
  blocking collectives: 0 us -> 43.5 us
  matrix products: 54.2 us -> 95 us
  other arithmetic: 24.6 us -> 0.02 us
  starting transfers between devices: 18.7 us -> 0.2 us
    all_to_all x3 -> x0, waiting for transfers between devices: 398 us -> none  [the longest x1 226 us: per_device(): lax.all_to_all(finished, 'exp', split_axis=0, concat_axis=0, tiled=True)]
    reduce_scatter x0 -> x2, waiting for transfers between devices: none -> 314 us  [the longest x1 281 us: per_device(): lax.psum_scatter(total.astype(jnp.bfloat16), 'exp', scatter_dimension=0,...]
    all_gather x3 -> x4, waiting for transfers between devices: 0.04 us -> 171 us  [the longest x1 171 us: per_device(): all_tokens = lax.all_gather(tokens, ('exp', 'x'), axis=0, tiled=True)]
    gather x3 -> x0, local copies, waits for them, and re-layouts: 53.1 us -> none  [the longest x2 32.6 us: per_device(): per_expert.append(extended[source_row].reshape(owners, capacity, width))]
    all_gather x0 -> x1, blocking collectives: none -> 43.5 us  [per_device(): all_weight = lax.all_gather(weight, ('exp', 'x'), axis=0, tiled=True)]
    dot_general x8 -> x6, matrix products: 54.2 us -> 95 us  [the longest x2 38.6 us: per_device(): done = jnp.dot(hidden, down[one], preferred_element_type=jnp.float32)]
    all_to_all x3 -> x0, starting transfers between devices: 18.6 us -> none  [the longest x1 7.28 us: per_device(): lax.all_to_all(member_sent, 'exp', split_axis=0, concat_axis=0, tiled=True)]
    reduce_sum x5 -> x1, other arithmetic: 14.5 us -> 0.02 us  [per_device(): jnp.sum(jnp.where(onehot, gate_fixed[:, :, None].astype(jnp.float32) / 65...]
  transfers between devices with their start and end apart: 6 -> 6, of which waited for: 2 -> 3; matrix products, arithmetic and copies ran while one was open for 16% -> 9% of each run, Pallas kernels for 0% -> 0%
where the time goes in v1:
time: 641 us
  waiting for transfers between devices  488 us (76%)
  matrix products  95 us (15%)
  blocking collectives  43.5 us (7%)
  between operations  13.6 us (2%)
    reduce_scatter x1, waiting for transfers between devices, per_device(): lax.psum_scatter(total.astype(jnp.bfloat16), 'exp', scatter_dimension=0,...  281 us
    all_gather x1, waiting for transfers between devices, per_device(): all_tokens = lax.all_gather(tokens, ('exp', 'x'), axis=0, tiled=True)  171 us
    all_gather x1, blocking collectives, per_device(): all_weight = lax.all_gather(weight, ('exp', 'x'), axis=0, tiled=True)  43.5 us
    dot_general x2, matrix products, per_device(): done = jnp.dot(hidden, down[one], preferred_element_type=jnp.float32)  38.6 us
    reduce_scatter x1, waiting for transfers between devices, per_device(): return lax.psum_scatter(part, 'x', scatter_dimension=0, tiled=True)  33.1 us
    dot_general x2, matrix products, per_device(): up_part = jnp.dot(all_tokens, up[one], preferred_element_type=jnp.float32)  28.9 us
    dot_general x2, matrix products, per_device(): jnp.dot(all_tokens, gate[one], preferred_element_type=jnp.float32)  27.6 us
  transfers between devices with their start and end apart: 6, of which 3 were waited for; matrix products, arithmetic and copies ran while one was open for 9% of the time, Pallas kernels for 0%

profile of v1, /device:TPU:0, one launch (start us, length us, event | category | flops | bytes accessed | tf_op | source)
XLA Modules:
  0.0 640.6 jit_solution(13082444013937959030)
XLA Ops:
  6.5 0.7 all-gather.7.cloned.1.call-update
  7.3 0.0 all-gather.5.cloned.1.call-start
  7.3 0.7 all-gather.5.cloned.1.call-update
  8.0 0.0 all-gather.9.cloned.1.call-start
  8.1 0.7 all-gather.9.cloned.1.call-update
  8.8 0.0 all-gather.11.cloned.1.call-start
  8.8 0.5 all-gather.11.cloned.1.call-update
  9.3 0.0 reduce-scatter.3.cloned.1.call-start
  9.4 0.0 copy-done
  9.4 43.5 %all_gather.15 = f32[2048,16]{0,1:T(8,128)S(1)} all-gather(f32[128,16]{0,1:T(8,128)S(1)} %select_reduce_fusion), channel_id=1, replica_groups=mesh['x'=2,'core'=2,'exp'=8] {'exp','x'}, dimensions={0}, use_global_device_ids=true | all-gather | bytes 139264 | tf_op jit(solution)/shard_map/all_gather | solution.py:17
  53.0 0.0 all-gather.7.cloned.1.call-done
  53.0 171.1 %all-gather.5.cloned.1.call-done = bf16[2048,4096]{1,0:T(8,128)(2,1)} async-done(((bf16[128,4096]{1,0:T(8,128)(2,1)}), bf16[2048,4096]{1,0:T(8,128)(2,1)}) %all-gather.5.cloned.1.call-update) | async-done | bytes 16777232 | tf_op jit(solution)/shard_map/all_gather | solution.py:16
  224.1 15.4 %fusion = f32[2048,384]{1,0:T(8,128)} fusion(bf16[2048,4096]{1,0:T(8,128)(2,1)} %all-gather.5.cloned.1.call-done, bf16[2,4096,384]{1,2,0:T(8,128)(2,1)} %all-gather.7.cloned.1.call-done), kind=kOutput, calls=%fused_computation.6 | convolution fusion | flops 6442450944 | bytes 23068672 | tf_op jit(solution)/shard_map/dot_general | solution.py:24
  239.5 12.2 %fusion.2 = f32[2048,384]{1,0:T(8,128)} fusion(bf16[2048,4096]{1,0:T(8,128)(2,1)S(1)} %copy-done.2, bf16[2,4096,384]{1,2,0:T(8,128)(2,1)} %all-gather.7.cloned.1.call-done), kind=kOutput, calls=%fused_computation.11 | convolution fusion | flops 6442450944 | bytes 23068672 | tf_op jit(solution)/shard_map/dot_general | solution.py:24
  251.7 15.9 %fusion.3 = bf16[2048,384]{1,0:T(8,128)(2,1)S(1)} fusion(bf16[2048,4096]{1,0:T(8,128)(2,1)} %all-gather.5.cloned.1.call-done, bf16[2,4096,384]{1,2,0:T(8,128)(2,1)} %all-gather.9.cloned.1.call-done, f32[2048,384]{1,0:T(8,128)} %fusion.2), kind=kOutput, calls=%fused_computation.12 | convolution fusion | flops 6447169536 | bytes 24641536 | tf_op jit(solution)/shard_map/dot_general | solution.py:25
  267.7 12.9 %fusion.4 = bf16[2048,384]{1,0:T(8,128)(2,1)S(1)} fusion(bf16[2048,4096]{1,0:T(8,128)(2,1)} %all-gather.5.cloned.1.call-done, bf16[2,4096,384]{1,2,0:T(8,128)(2,1)S(1)} %copy-done.3, f32[2048,384]{1,0:T(8,128)S(1)} %copy-done.4), kind=kOutput, calls=%fused_computation.13 | convolution fusion | flops 6447169536 | bytes 24641536 | tf_op jit(solution)/shard_map/dot_general | solution.py:25
  280.6 0.0 all-gather.11.cloned.1.call-done
  280.6 16.4 %fusion.1 = f32[2048,4096]{1,0:T(8,128)} fusion(bf16[2048,384]{1,0:T(8,128)(2,1)S(1)} %fusion.3, bf16[2,384,4096]{2,1,0:T(8,128)(2,1)} %all-gather.11.cloned.1.call-done), kind=kOutput, calls=%fused_computation.8 | convolution fusion | flops 6442450944 | bytes 38273024 | tf_op jit(solution)/shard_map/dot_general | solution.py:27
  297.0 22.2 %add_convert_fusion = bf16[2048,4096]{1,0:T(8,128)(2,1)} fusion(f32[2048,4096]{1,0:T(8,128)} %fusion.1, f32[2048]{0:T(1024)S(1)} %bitcast.31, f32[2048]{0:T(1024)S(1)} %bitcast.30, bf16[2048,384]{1,0:T(8,128)(2,1)S(1)} %fusion.4, bf16[2,384,4096]{2,1,0:T(8,128)(2,1)} %all-gather.11.cloned.1.call-done), kind=kOutput, calls=%fused_computation | convolution fusion | flops 6476005376 | bytes 55066624 | tf_op jit(solution)/shard_map/dot_general | solution.py:27
  319.2 0.0 reduce-scatter.3.cloned.1.call-update
  319.2 0.0 reduce-scatter.5.cloned.1.call-start
  319.3 281.3 %reduce-scatter.3.cloned.1.call-done = bf16[256,4096]{1,0:T(8,128)(2,1)} async-done(((bf16[2048,4096]{1,0:T(8,128)(2,1)}), bf16[256,4096]{1,0:T(8,128)(2,1)}) %reduce-scatter.3.cloned.1.call-update) | async-done | bytes 2097168 | tf_op jit(solution)/shard_map/reduce_scatter | solution.py:30
  600.6 0.0 reduce-scatter.5.cloned.1.call-update
  600.6 33.1 %reduce-scatter.5.cloned.1.call-done = bf16[128,4096]{1,0:T(8,128)(2,1)} async-done(((bf16[256,4096]{1,0:T(8,128)(2,1)}), bf16[128,4096]{1,0:T(8,128)(2,1)}) %reduce-scatter.5.cloned.1.call-update) | async-done | bytes 1048592 | tf_op jit(solution)/shard_map/reduce_scatter | solution.py:33
  (14 shorter events, 0.1 us)
Async XLA Ops:
  6.5 46.5 %all-gather.7.cloned.1.call-start = ((), (), s32[]{:S(2)}) async-start(), calls=%async_computation.3 | async-start | bytes 9437184 | tf_op jit(solution)/shard_map/all_gather | solution.py:18
  7.3 216.8 %all-gather.5.cloned.1.call-start = ((), (), s32[]{:S(2)}) async-start(), calls=%async_computation.2 | async-start | bytes 17825792 | tf_op jit(solution)/shard_map/all_gather | solution.py:16
  8.0 1.4 copy-start
  8.0 1.4 copy-start.1
  8.0 243.7 %all-gather.9.cloned.1.call-start = ((), (), s32[]{:S(2)}) async-start(), calls=%async_computation.4 | async-start | bytes 9437184 | tf_op jit(solution)/shard_map/all_gather | solution.py:19
  8.8 271.9 %all-gather.11.cloned.1.call-start = ((), (), s32[]{:S(2)}) async-start(), calls=%async_computation.5 | async-start | bytes 9437184 | tf_op jit(solution)/shard_map/all_gather | solution.py:20
  9.3 591.3 %reduce-scatter.3.cloned.1.call-start = ((), (), s32[]{:S(2)}) async-start(), calls=%async_computation.6 | async-start | bytes 18874368 | tf_op jit(solution)/shard_map/reduce_scatter | solution.py:30
  224.1 15.4 %copy-start.2 = (bf16[2048,4096]{1,0:T(8,128)(2,1)S(1)}, bf16[2048,4096]{1,0:T(8,128)(2,1)}, u32[]{:S(2)}) copy-start(bf16[2048,4096]{1,0:T(8,128)(2,1)} %all-gather.5.cloned.1.call-done) | copy-start | bytes 50331652
  251.7 15.9 %copy-start.3 = (bf16[2,4096,384]{1,2,0:T(8,128)(2,1)S(1)}, bf16[2,4096,384]{1,2,0:T(8,128)(2,1)}, u32[]{:S(2)}) copy-start(bf16[2,4096,384]{1,2,0:T(8,128)(2,1)} %all-gather.9.cloned.1.call-done) | copy-start | bytes 18874372
  251.7 16.0 %copy-start.4 = (f32[2048,384]{1,0:T(8,128)S(1)}, f32[2048,384]{1,0:T(8,128)}, u32[]{:S(2)}) copy-start(f32[2048,384]{1,0:T(8,128)} %fusion) | copy-start | bytes 9437188
  319.2 314.5 %reduce-scatter.5.cloned.1.call-start = ((), (), s32[]{:S(2)}) async-start(), calls=%async_computation.7 | async-start | bytes 3145728 | tf_op jit(solution)/shard_map/reduce_scatter | solution.py:33
Sparse Core Ops, SparseCore 0:
  8.9 19.4 all-gather.6
  31.2 192.8 all-gather.4
  225.6 14.9 all-gather.8
  242.0 17.9 all-gather.10
  319.3 281.2 reduce-scatter.2
  602.8 30.8 reduce-scatter.4

commit v2 on v1

v2 whole, which is shorter than its diff:
```python
import jax
import jax.numpy as jnp
from jax import lax
from jax.sharding import Mesh
from jax.sharding import PartitionSpec as P

EXPERTS = 16


def per_device(tokens, expert_ids, gate_fixed, w_gate, w_up, w_down):
    local = w_gate.shape[0]
    onehot = expert_ids[:, :, None] == jnp.arange(EXPERTS, dtype=jnp.int32)[None, None, :]
    weight = jnp.sum(
        jnp.where(onehot, gate_fixed[:, :, None].astype(jnp.float32) / 65536.0, 0.0), axis=1
    )
    chips = lax.axis_size("x")
    blocks, axes = [(w_gate, w_up, w_down)], ("x", "core")
    if chips == 2:
        swap, axes = [(0, 1), (1, 0)], ("core",)
        blocks.append(tuple(lax.ppermute(panel, "x", swap) for panel in blocks[0]))
    all_tokens = lax.all_gather(tokens, "exp", axis=0, tiled=True)
    all_weight = lax.all_gather(weight, "exp", axis=0, tiled=True)
    mine = lax.dynamic_slice_in_dim(all_weight, lax.axis_index("exp") * local, local, axis=1)
    total = None
    for w_gate, w_up, w_down in blocks:
        gate = lax.all_gather(w_gate, axes, axis=2, tiled=True)
        up = lax.all_gather(w_up, axes, axis=2, tiled=True)
        down = lax.all_gather(w_down, axes, axis=1, tiled=True)
        for one in range(local):
            gate_part = jnp.dot(all_tokens, gate[one], preferred_element_type=jnp.float32)
            up_part = jnp.dot(all_tokens, up[one], preferred_element_type=jnp.float32)
            hidden = (jax.nn.silu(gate_part) * up_part).astype(jnp.bfloat16)
            done = jnp.dot(hidden, down[one], preferred_element_type=jnp.float32)
            term = mine[:, one : one + 1] * done
            total = term if total is None else total + term
    return lax.psum_scatter(
        total.astype(jnp.bfloat16), "exp", scatter_dimension=0, tiled=True
    )


def solution(mesh):
    grp, exp = mesh.shape["grp"], mesh.shape["exp"]
    split = Mesh(mesh.devices.reshape(grp // 2, 2, exp), ("x", "core", "exp"))
    rows = P(("x", "core", "exp"), None)
    in_specs = (
        rows,
        rows,
        rows,
        P("exp", None, ("x", "core")),
        P("exp", None, ("x", "core")),
        P("exp", ("x", "core"), None),
    )
    return jax.shard_map(
        per_device, mesh=split, in_specs=in_specs, out_specs=rows, check_vma=False
    )
```

time: 641 us -> 493 us (0.77)
  waiting for transfers between devices: 488 us -> 325 us
  matrix products: 95 us -> 116 us
  blocking collectives: 43.5 us -> 30.8 us
    ppermute x0 -> x3, waiting for transfers between devices: none -> 172 us  [per_device(): lax.ppermute(panel, 'x', swap)]
    all_gather x4 -> x7, waiting for transfers between devices: 171 us -> 0.06 us  [the longest x2 0.04 us: per_device(): gate = lax.all_gather(w_gate, axes, axis=2, tiled=True)]
    reduce_scatter x1, waiting for transfers between devices: 281 us -> 150 us  [per_device(): lax.psum_scatter(total.astype(jnp.bfloat16), 'exp', scatter_dimension=0,...]
    dot_general x2 -> x4, matrix products: 38.6 us -> 73 us  [per_device(): done = jnp.dot(hidden, down[one], preferred_element_type=jnp.float32)]
    reduce_scatter x1 -> x0, waiting for transfers between devices: 33.1 us -> none  [per_device(): return lax.psum_scatter(part, 'x', scatter_dimension=0, tiled=True)]
    dot_general x2, matrix products: 28.9 us -> 16 us  [per_device(): up_part = jnp.dot(all_tokens, up[one], preferred_element_type=jnp.float32)]
    all_gather x1, blocking collectives: 43.5 us -> 30.8 us  [per_device(): all_weight = lax.all_gather(weight, 'exp', axis=0, tiled=True)]
    dot_general x2 -> x3, matrix products: 27.6 us -> 27.4 us  [per_device(): jnp.dot(all_tokens, gate[one], preferred_element_type=jnp.float32)]
  transfers between devices with their start and end apart: 6 -> 11, of which waited for: 3 -> 4; matrix products, arithmetic and copies ran while one was open for 9% -> 16% of each run, Pallas kernels for 0% -> 0%
where the time goes in v2:
time: 493 us
  waiting for transfers between devices  325 us (66%)
  matrix products  116 us (24%)
  blocking collectives  30.8 us (6%)
  between operations  13.6 us (3%)
  starting transfers between devices  6.5 us (1%)
    ppermute x3, waiting for transfers between devices, per_device(): lax.ppermute(panel, 'x', swap)  172 us
    reduce_scatter x1, waiting for transfers between devices, per_device(): lax.psum_scatter(total.astype(jnp.bfloat16), 'exp', scatter_dimension=0,...  150 us
    dot_general x4, matrix products, per_device(): done = jnp.dot(hidden, down[one], preferred_element_type=jnp.float32)  73 us
    all_gather x1, blocking collectives, per_device(): all_weight = lax.all_gather(weight, 'exp', axis=0, tiled=True)  30.8 us
    dot_general x3, matrix products, per_device(): jnp.dot(all_tokens, gate[one], preferred_element_type=jnp.float32)  27.4 us
    dot_general x2, matrix products, per_device(): up_part = jnp.dot(all_tokens, up[one], preferred_element_type=jnp.float32)  16 us
  transfers between devices with their start and end apart: 11, of which 4 were waited for; matrix products, arithmetic and copies ran while one was open for 16% of the time, Pallas kernels for 0%

profile of v2, /device:TPU:0, one launch (start us, length us, event | category | flops | bytes accessed | tf_op | source)
XLA Modules:
  0.0 492.8 jit_solution(1471973868300645789)
XLA Ops:
  6.5 0.7 all-gather.10.cloned.1.call-update
  7.3 0.7 all-gather.8.cloned.1.call-update
  8.1 3.0 collective-permute-start.1
  11.1 68.4 %collective-permute-done.1 = bf16[2,4096,192]{1,2,0:T(8,128)(2,1)} collective-permute-done((bf16[2,4096,192]{1,2,0:T(8,128)(2,1)}, bf16[2,4096,192]{1,2,0:T(8,128)(2,1)}, u32[]{:S(2)}, u32[]{:S(2)}) %collective-permute-start.1) | collective-permute-done | bytes 3145760 | tf_op jit(solution)/shard_map/ppermute | solution.py:20
  79.6 1.8 collective-permute-start
  81.4 67.7 %collective-permute-done = bf16[2,4096,192]{1,2,0:T(8,128)(2,1)} collective-permute-done((bf16[2,4096,192]{1,2,0:T(8,128)(2,1)S(1)}, bf16[2,4096,192]{1,2,0:T(8,128)(2,1)}, u32[]{:S(2)}, u32[]{:S(2)}) %collective-permute-start) | collective-permute-done | bytes 3145760 | tf_op jit(solution)/shard_map/ppermute | solution.py:20
  149.1 0.5 all-gather.12.cloned.1.call-update
  149.7 0.5 all-gather.14.cloned.1.call-update
  150.2 0.0 all-gather.20.cloned.1.call-start
  150.3 0.7 copy-done.2
  150.9 1.4 collective-permute-start.2
  152.4 30.8 %all_gather.24 = f32[1024,16]{0,1:T(8,128)S(1)} all-gather(f32[128,16]{0,1:T(8,128)S(1)} %select_reduce_fusion), channel_id=1, replica_groups=mesh['x'=2,'core'=2,'exp'=8] {'exp'}, dimensions={0}, use_global_device_ids=true | all-gather | bytes 73728 | tf_op jit(solution)/shard_map/all_gather | solution.py:22
  183.2 36.2 %collective-permute-done.2 = bf16[2,192,4096]{2,1,0:T(8,128)(2,1)} collective-permute-done((bf16[2,192,4096]{2,1,0:T(8,128)(2,1)S(1)}, bf16[2,192,4096]{2,1,0:T(8,128)(2,1)}, u32[]{:S(2)}, u32[]{:S(2)}) %collective-permute-start.2) | collective-permute-done | bytes 3145760 | tf_op jit(solution)/shard_map/ppermute | solution.py:20
  219.4 0.0 reduce-scatter.2.cloned.1.call-start
  219.5 11.8 %fusion.7 = f32[1024,384]{1,0:T(8,128)} fusion(bf16[1024,4096]{1,0:T(8,128)(2,1)} %all-gather.8.cloned.1.call-done, bf16[2,4096,384]{1,2,0:T(8,128)(2,1)} %all-gather.10.cloned.1.call-done), kind=kOutput, calls=%fused_computation.17 | convolution fusion | flops 3221225472 | bytes 13107200 | tf_op jit(solution)/shard_map/dot_general | solution.py:30
  231.3 5.6 %fusion.10 = f32[1024,384]{1,0:T(8,128)} fusion(bf16[1024,4096]{1,0:T(8,128)(2,1)S(1)} %copy-done, bf16[2,4096,384]{1,2,0:T(8,128)(2,1)S(1)} %copy-done.5), kind=kOutput, calls=%fused_computation.23 | convolution fusion | flops 3221225472 | bytes 13107200 | tf_op jit(solution)/shard_map/dot_general | solution.py:30
  237.0 8.2 %fusion = f32[1024,384]{1,0:T(8,128)S(1)} fusion(bf16[1024,4096]{1,0:T(8,128)(2,1)} %all-gather.8.cloned.1.call-done, bf16[2,4096,384]{1,2,0:T(8,128)(2,1)} %all-gather.18.cloned.1.call-done), kind=kOutput, calls=%fused_computation.3 | convolution fusion | flops 3221225472 | bytes 13107200 | tf_op jit(solution)/shard_map/dot_general | solution.py:31
  245.2 7.8 %fusion.3 = f32[1024,384]{1,0:T(8,128)S(1)} fusion(bf16[1024,4096]{1,0:T(8,128)(2,1)} %all-gather.8.cloned.1.call-done, bf16[2,4096,384]{1,2,0:T(8,128)(2,1)S(1)} %copy-done.6), kind=kOutput, calls=%fused_computation.9 | convolution fusion | flops 3221225472 | bytes 13107200 | tf_op jit(solution)/shard_map/dot_general | solution.py:31
  253.0 10.0 %fusion.4 = f32[1024,384]{1,0:T(8,128)} fusion(bf16[1024,4096]{1,0:T(8,128)(2,1)} %all-gather.8.cloned.1.call-done, bf16[2,4096,384]{1,2,0:T(8,128)(2,1)} %all-gather.16.cloned.1.call-done), kind=kOutput, calls=%fused_computation.11 | convolution fusion | flops 3221225472 | bytes 13107200 | tf_op jit(solution)/shard_map/dot_general | solution.py:30
  263.0 16.6 %fusion.8 = f32[1024,4096]{1,0:T(8,128)} fusion(bf16[2,384,4096]{2,1,0:T(8,128)(2,1)} %all-gather.14.cloned.1.call-done, f32[1024,384]{1,0:T(8,128)} %fusion.10, bf16[1024,4096]{1,0:T(8,128)(2,1)} %all-gather.8.cloned.1.call-done, bf16[2,4096,384]{1,2,0:T(8,128)(2,1)} %all-gather.12.cloned.1.call-done), kind=kOutput, calls=%fused_computation.19 | convolution fusion | flops 6444810240 | bytes 33030144 | tf_op jit(solution)/shard_map/dot_general | solution.py:33
  279.6 16.9 %fusion.5 = f32[1024,4096]{1,0:T(8,128)} fusion(bf16[2,384,4096]{2,1,0:T(8,128)(2,1)} %all-gather.14.cloned.1.call-done, f32[1024,384]{1,0:T(8,128)} %fusion.7, bf16[1024,4096]{1,0:T(8,128)(2,1)} %all-gather.8.cloned.1.call-done, bf16[2,4096,384]{1,2,0:T(8,128)(2,1)} %all-gather.12.cloned.1.call-done), kind=kOutput, calls=%fused_computation.13 | convolution fusion | flops 6444810240 | bytes 33030144 | tf_op jit(solution)/shard_map/dot_general | solution.py:33
  296.5 12.6 %fusion.2 = f32[1024,4096]{1,0:T(8,128)} fusion(bf16[2,384,4096]{2,1,0:T(8,128)(2,1)} %all-gather.20.cloned.1.call-done, f32[1024,384]{1,0:T(8,128)S(1)} %fusion.3, f32[1024,384]{1,0:T(8,128)} %fusion.4), kind=kOutput, calls=%fused_computation.7 | convolution fusion | flops 3223584768 | bytes 23068672 | tf_op jit(solution)/shard_map/dot_general | solution.py:33
  309.1 26.9 %add_convert_fusion = bf16[1024,4096]{1,0:T(8,128)(2,1)} fusion(f32[1024,4096]{1,0:T(8,128)} %fusion.2, f32[1024,4096]{1,0:T(8,128)} %fusion.5, f32[1024,4096]{1,0:T(8,128)} %fusion.8, f32[1024]{0:T(1024)S(1)} %bitcast.59, f32[1024]{0:T(1024)S(1)} %bitcast.58, bf16[2,384,4096]{2,1,0:T(8,128)(2,1)} %all-gather.20.cloned.1.call-done, f32[1024,384]{1,0:T(8,128)S(1)} %fusion, ...), kind=kOutput, calls=%fused_computation | convolution fusion | flops 6478364672 | bytes 74981376 | tf_op jit(solution)/shard_map/dot_general | solution.py:33
  336.0 150.0 %reduce-scatter.2.cloned.1.call-done = bf16[128,4096]{1,0:T(8,128)(2,1)} async-done(((bf16[1024,4096]{1,0:T(8,128)(2,1)}), bf16[128,4096]{1,0:T(8,128)(2,1)}) %reduce-scatter.2.cloned.1.call-update) | async-done | bytes 1048592 | tf_op jit(solution)/shard_map/reduce_scatter | solution.py:36
  (33 shorter events, 0.4 us)
Async XLA Ops:
  6.5 73.0 %copy-start.1 = (bf16[2,4096,192]{1,2,0:T(8,128)(2,1)S(1)}, bf16[2,4096,192]{1,2,0:T(8,128)(2,1)}, u32[]{:S(2)}) copy-start(bf16[2,4096,192]{1,2,0:T(8,128)(2,1)} %param.9) | copy-start | bytes 9437188
  6.5 212.9 %all-gather.10.cloned.1.call-start = ((), (), s32[]{:S(2)}) async-start(), calls=%async_computation.2 | async-start | bytes 9437184 | tf_op jit(solution)/shard_map/all_gather | solution.py:26
  7.3 212.2 %all-gather.8.cloned.1.call-start = ((), (), s32[]{:S(2)}) async-start(), calls=%async_computation.1 | async-start | bytes 9437184 | tf_op jit(solution)/shard_map/all_gather | solution.py:21
  8.0 229.0 %all-gather.18.cloned.1.call-start = ((), (), s32[]{:S(2)}) async-start(), calls=%async_computation.6 | async-start | bytes 9437184 | tf_op jit(solution)/shard_map/all_gather | solution.py:27
  8.1 71.4 %collective-permute-start.1 = (bf16[2,4096,192]{1,2,0:T(8,128)(2,1)}, bf16[2,4096,192]{1,2,0:T(8,128)(2,1)}, u32[]{:S(2)}, u32[]{:S(2)}) collective-permute-start(bf16[2,4096,192]{1,2,0:T(8,128)(2,1)} %param.10), channel_id=1, source_target_pairs={{0,16},{16,0},{1,17},{17,1},{2,18},{18,2},{3,19},{19,3},{4,20},{20... | collective-permute-start | bytes 9437192 | tf_op jit(solution)/shard_map/ppermute | solution.py:20
  79.5 72.9 %copy-start.3 = (s32[128,8]{0,1:T(8,128)S(1)}, s32[128,8]{0,1:T(8,128)}, u32[]{:S(2)}) copy-start(s32[128,8]{0,1:T(8,128)} %param.8) | copy-start | bytes 12292
  79.5 72.9 %copy-start.4 = (s32[128,8]{0,1:T(8,128)S(1)}, s32[128,8]{0,1:T(8,128)}, u32[]{:S(2)}) copy-start(s32[128,8]{0,1:T(8,128)} %param.7) | copy-start | bytes 12292
  79.5 173.5 %all-gather.16.cloned.1.call-start = ((), (), s32[]{:S(2)}) async-start(), calls=%async_computation.5 | async-start | bytes 9437184 | tf_op jit(solution)/shard_map/all_gather | solution.py:26
  79.6 69.5 %collective-permute-start = (bf16[2,4096,192]{1,2,0:T(8,128)(2,1)S(1)}, bf16[2,4096,192]{1,2,0:T(8,128)(2,1)}, u32[]{:S(2)}, u32[]{:S(2)}) collective-permute-start(bf16[2,4096,192]{1,2,0:T(8,128)(2,1)S(1)} %copy-done.1), channel_id=1, source_target_pairs={{0,16},{16,0},{1,17},{17,1},{2,18},{18,2},{3,19},{19,3},{4,20},{20... | collective-permute-start | bytes 9437192 | tf_op jit(solution)/shard_map/ppermute | solution.py:20
  149.0 1.9 copy-start.2
  149.0 113.9 %all-gather.12.cloned.1.call-start = ((), (), s32[]{:S(2)}) async-start(), calls=%async_computation.3 | async-start | bytes 9437184 | tf_op jit(solution)/shard_map/all_gather | solution.py:27
  149.6 113.4 %all-gather.14.cloned.1.call-start = ((), (), s32[]{:S(2)}) async-start(), calls=%async_computation.4 | async-start | bytes 9437184 | tf_op jit(solution)/shard_map/all_gather | solution.py:28
  150.2 146.3 %all-gather.20.cloned.1.call-start = ((), (), s32[]{:S(2)}) async-start(), calls=%async_computation.7 | async-start | bytes 9437184 | tf_op jit(solution)/shard_map/all_gather | solution.py:28
  150.9 68.5 %collective-permute-start.2 = (bf16[2,192,4096]{2,1,0:T(8,128)(2,1)S(1)}, bf16[2,192,4096]{2,1,0:T(8,128)(2,1)}, u32[]{:S(2)}, u32[]{:S(2)}) collective-permute-start(bf16[2,192,4096]{2,1,0:T(8,128)(2,1)S(1)} %copy-done.2), channel_id=1, source_target_pairs={{0,16},{16,0},{1,17},{17,1},{2,18},{18,2},{3,19},{19,3},{4,20},{20... | collective-permute-start | bytes 9437192 | tf_op jit(solution)/shard_map/ppermute | solution.py:20
  219.4 266.6 %reduce-scatter.2.cloned.1.call-start = ((), (), s32[]{:S(2)}) async-start(), calls=%async_computation.8 | async-start | bytes 9437184 | tf_op jit(solution)/shard_map/reduce_scatter | solution.py:36
  219.5 11.8 %copy-start = (bf16[1024,4096]{1,0:T(8,128)(2,1)S(1)}, bf16[1024,4096]{1,0:T(8,128)(2,1)}, u32[]{:S(2)}) copy-start(bf16[1024,4096]{1,0:T(8,128)(2,1)} %all-gather.8.cloned.1.call-done) | copy-start | bytes 25165828
  219.5 11.8 %copy-start.5 = (bf16[2,4096,384]{1,2,0:T(8,128)(2,1)S(1)}, bf16[2,4096,384]{1,2,0:T(8,128)(2,1)}, u32[]{:S(2)}) copy-start(bf16[2,4096,384]{1,2,0:T(8,128)(2,1)} %all-gather.10.cloned.1.call-done) | copy-start | bytes 18874372
  237.0 8.2 %copy-start.6 = (bf16[2,4096,384]{1,2,0:T(8,128)(2,1)S(1)}, bf16[2,4096,384]{1,2,0:T(8,128)(2,1)}, u32[]{:S(2)}) copy-start(bf16[2,4096,384]{1,2,0:T(8,128)(2,1)} %all-gather.18.cloned.1.call-done) | copy-start | bytes 18874372
Sparse Core Ops, SparseCore 0:
  8.9 19.4 all-gather.9
  30.5 126.1 all-gather.7
  158.3 14.9 all-gather.17
  174.6 17.9 all-gather.15
  194.0 17.9 all-gather.11
  213.4 17.9 all-gather.13
  232.9 17.9 all-gather.19
  336.1 149.7 reduce-scatter.1

commit v3 on v2

--- a/solution.py
+++ b/solution.py
@@ -26,13 +26,18 @@
         gate = lax.all_gather(w_gate, axes, axis=2, tiled=True)
         up = lax.all_gather(w_up, axes, axis=2, tiled=True)
         down = lax.all_gather(w_down, axes, axis=1, tiled=True)
+        hidden = []
         for one in range(local):
             gate_part = jnp.dot(all_tokens, gate[one], preferred_element_type=jnp.float32)
             up_part = jnp.dot(all_tokens, up[one], preferred_element_type=jnp.float32)
-            hidden = (jax.nn.silu(gate_part) * up_part).astype(jnp.bfloat16)
-            done = jnp.dot(hidden, down[one], preferred_element_type=jnp.float32)
-            term = mine[:, one : one + 1] * done
-            total = term if total is None else total + term
+            value = jax.nn.silu(gate_part) * up_part * mine[:, one : one + 1]
+            hidden.append(value.astype(jnp.bfloat16))
+        term = jnp.dot(
+            jnp.concatenate(hidden, axis=1),
+            down.reshape(-1, down.shape[2]),
+            preferred_element_type=jnp.float32,
+        )
+        total = term if total is None else total + term
     return lax.psum_scatter(
         total.astype(jnp.bfloat16), "exp", scatter_dimension=0, tiled=True
     )

time: 493 us -> 470 us (0.953)
  matrix products: 116 us -> 90 us
    dot_general x4 -> x2, matrix products: 73 us -> 27.8 us  [per_device(): jnp.dot(jnp.concatenate(hidden, axis=1), down.reshape(-1, down.shape[2]),...]
    dot_general x2 -> x4, matrix products: 16 us -> 32.5 us  [per_device(): up_part = jnp.dot(all_tokens, up[one], preferred_element_type=jnp.float32)]
    dot_general x3 -> x4, matrix products: 27.4 us -> 29.7 us  [per_device(): jnp.dot(all_tokens, gate[one], preferred_element_type=jnp.float32)]
where the time goes in v3:
time: 470 us
  waiting for transfers between devices  325 us (69%)
  matrix products  90 us (19%)
  blocking collectives  30.8 us (7%)
  between operations  13.7 us (3%)
  starting transfers between devices  6.38 us (1%)
    ppermute x3, waiting for transfers between devices, per_device(): lax.ppermute(panel, 'x', swap)  172 us
    reduce_scatter x1, waiting for transfers between devices, per_device(): lax.psum_scatter(total.astype(jnp.bfloat16), 'exp', scatter_dimension=0,...  151 us
    dot_general x4, matrix products, per_device(): up_part = jnp.dot(all_tokens, up[one], preferred_element_type=jnp.float32)  32.5 us
    all_gather x1, blocking collectives, per_device(): all_weight = lax.all_gather(weight, 'exp', axis=0, tiled=True)  30.8 us
    dot_general x4, matrix products, per_device(): jnp.dot(all_tokens, gate[one], preferred_element_type=jnp.float32)  29.7 us
    dot_general x2, matrix products, per_device(): jnp.dot(jnp.concatenate(hidden, axis=1), down.reshape(-1, down.shape[2]),...  27.8 us
  transfers between devices with their start and end apart: 11, of which 4 were waited for; matrix products, arithmetic and copies ran while one was open for 16% of the time, Pallas kernels for 0%

profile of v3, /device:TPU:0, one launch (start us, length us, event | category | flops | bytes accessed | tf_op | source)
XLA Modules:
  0.0 469.8 jit_solution(15368799715596896650)
XLA Ops:
  6.5 0.7 all-gather.10.cloned.1.call-update
  7.3 0.7 all-gather.8.cloned.1.call-update
  8.4 2.9 collective-permute-start
  11.4 68.2 %collective-permute-done = bf16[2,4096,192]{1,2,0:T(8,128)(2,1)} collective-permute-done((bf16[2,4096,192]{1,2,0:T(8,128)(2,1)S(1)}, bf16[2,4096,192]{1,2,0:T(8,128)(2,1)}, u32[]{:S(2)}, u32[]{:S(2)}) %collective-permute-start) | collective-permute-done | bytes 3145760 | tf_op jit(solution)/shard_map/ppermute | solution.py:20
  80.2 0.5 all-gather.14.cloned.1.call-update
  80.8 0.7 copy-done.1
  81.5 1.7 collective-permute-start.1
  83.2 67.6 %collective-permute-done.1 = bf16[2,4096,192]{1,2,0:T(8,128)(2,1)} collective-permute-done((bf16[2,4096,192]{1,2,0:T(8,128)(2,1)S(1)}, bf16[2,4096,192]{1,2,0:T(8,128)(2,1)}, u32[]{:S(2)}, u32[]{:S(2)}) %collective-permute-start.1) | collective-permute-done | bytes 3145760 | tf_op jit(solution)/shard_map/ppermute | solution.py:20
  150.9 1.8 copy-done.2
  152.8 1.4 collective-permute-start.2
  154.2 30.8 %all_gather.27 = f32[1024,16]{0,1:T(8,128)S(1)} all-gather(f32[128,16]{0,1:T(8,128)S(1)} %select_reduce_fusion), channel_id=1, replica_groups=mesh['x'=2,'core'=2,'exp'=8] {'exp'}, dimensions={0}, use_global_device_ids=true | all-gather | bytes 73728 | tf_op jit(solution)/shard_map/all_gather | solution.py:22
  185.1 36.2 %collective-permute-done.2 = bf16[2,192,4096]{2,1,0:T(8,128)(2,1)} collective-permute-done((bf16[2,192,4096]{2,1,0:T(8,128)(2,1)S(1)}, bf16[2,192,4096]{2,1,0:T(8,128)(2,1)}, u32[]{:S(2)}, u32[]{:S(2)}) %collective-permute-start.2) | collective-permute-done | bytes 3145760 | tf_op jit(solution)/shard_map/ppermute | solution.py:20
  221.4 10.7 %fusion.5 = f32[1024,384]{0,1:T(8,128)} fusion(bf16[1024,4096]{1,0:T(8,128)(2,1)} %all-gather.8.cloned.1.call-done, bf16[2,4096,384]{1,2,0:T(8,128)(2,1)} %all-gather.10.cloned.1.call-done), kind=kOutput, calls=%fused_computation.12 | convolution fusion | flops 3221225472 | bytes 13107200 | tf_op jit(solution)/shard_map/dot_general | solution.py:31
  232.0 0.8 copy-done.6
  232.9 4.6 fusion.7
  237.5 7.2 %fusion.1 = f32[1024,384]{0,1:T(8,128)S(1)} fusion(bf16[1024,4096]{1,0:T(8,128)(2,1)} %all-gather.8.cloned.1.call-done, bf16[2,4096,384]{1,2,0:T(8,128)(2,1)} %all-gather.16.cloned.1.call-done), kind=kOutput, calls=%fused_computation.4 | convolution fusion | flops 3221225472 | bytes 13107200 | tf_op jit(solution)/shard_map/dot_general | solution.py:31
  244.8 9.5 %multiply_convert_fusion.3 = bf16[1024,384]{0,1:T(8,128)(2,1)S(1)} fusion(f32[1024,384]{0,1:T(8,128)} %fusion.7, bf16[1024,4096]{1,0:T(8,128)(2,1)} %all-gather.8.cloned.1.call-done, bf16[2,4096,384]{1,2,0:T(8,128)(2,1)} %all-gather.12.cloned.1.call-done, f32[1024]{0:T(1024)S(1)} %bitcast.47), kind=kOutput, calls=%fused_computation.27 | convolution fusion | flops 3223977984 | bytes 13897728 | tf_op jit(solution)/shard_map/dot_general | solution.py:32
  254.3 7.2 %fusion.3 = f32[1024,384]{0,1:T(8,128)} fusion(bf16[1024,4096]{1,0:T(8,128)(2,1)} %all-gather.8.cloned.1.call-done, bf16[2,4096,384]{1,2,0:T(8,128)(2,1)S(1)} %copy-done.7), kind=kOutput, calls=%fused_computation.8 | convolution fusion | flops 3221225472 | bytes 13107200 | tf_op jit(solution)/shard_map/dot_general | solution.py:31
  261.5 7.0 %multiply_convert_fusion.2 = bf16[1024,384]{0,1:T(8,128)(2,1)S(1)} fusion(f32[1024,384]{0,1:T(8,128)S(1)} %copy-done.11, bf16[1024,4096]{1,0:T(8,128)(2,1)} %all-gather.8.cloned.1.call-done, bf16[2,4096,384]{1,2,0:T(8,128)(2,1)S(1)} %copy-done.8, f32[1024]{0:T(1024)S(1)} %bitcast.49), kind=kOutput, calls=%fused_computation.26 | convolution fusion | flops 3223977984 | bytes 13897728 | tf_op jit(solution)/shard_map/dot_general | solution.py:32
  268.5 13.3 %fusion.8 = f32[1024,4096]{1,0:T(8,128)} fusion(bf16[768,4096]{1,0:T(8,128)(2,1)} %bitcast.46, bf16[1024,384]{0,1:T(8,128)(2,1)S(1)} %multiply_convert_fusion.2, bf16[1024,384]{0,1:T(8,128)(2,1)S(1)} %multiply_convert_fusion.3), kind=kOutput, calls=%fused_computation.17 | convolution fusion | flops 6445596672 | bytes 24641536 | tf_op jit(solution)/shard_map/dot_general | solution.py:35
  281.8 8.9 %multiply_convert_fusion = bf16[1024,384]{0,1:T(8,128)(2,1)} fusion(f32[1024,384]{0,1:T(8,128)S(1)} %fusion.1, f32[1024]{0:T(1024)S(1)} %bitcast.50, bf16[1024,4096]{1,0:T(8,128)(2,1)} %all-gather.8.cloned.1.call-done, bf16[2,4096,384]{1,2,0:T(8,128)(2,1)} %all-gather.18.cloned.1.call-done), kind=kOutput, calls=%fused_computation.24 | convolution fusion | flops 3223977984 | bytes 13897728 | tf_op jit(solution)/shard_map/dot_general | solution.py:32
  290.8 7.1 %multiply_convert_fusion.1 = bf16[1024,384]{0,1:T(8,128)(2,1)S(1)} fusion(f32[1024,384]{0,1:T(8,128)S(1)} %copy-done.10, f32[1024]{0:T(1024)S(1)} %bitcast.48, bf16[1024,4096]{1,0:T(8,128)(2,1)} %all-gather.8.cloned.1.call-done, bf16[2,4096,384]{1,2,0:T(8,128)(2,1)S(1)} %copy-done.9), kind=kOutput, calls=%fused_computation.25 | convolution fusion | flops 3223977984 | bytes 13897728 | tf_op jit(solution)/shard_map/dot_general | solution.py:32
  297.9 14.5 %add_convert_fusion = bf16[1024,4096]{1,0:T(8,128)(2,1)} fusion(f32[1024,4096]{1,0:T(8,128)} %fusion.8, bf16[768,4096]{1,0:T(8,128)(2,1)} %bitcast.51, bf16[1024,384]{0,1:T(8,128)(2,1)S(1)} %copy-done.12, bf16[1024,384]{0,1:T(8,128)(2,1)S(1)} %multiply_convert_fusion.1), kind=kOutput, calls=%fused_computation | convolution fusion | flops 6453985280 | bytes 33030144 | tf_op jit(solution)/shard_map/dot_general | solution.py:35
  312.4 150.6 %reduce-scatter.2.cloned.1.call-done = bf16[128,4096]{1,0:T(8,128)(2,1)} async-done(((bf16[1024,4096]{1,0:T(8,128)(2,1)}), bf16[128,4096]{1,0:T(8,128)(2,1)}) %reduce-scatter.2.cloned.1.call-update) | async-done | bytes 1048592 | tf_op jit(solution)/shard_map/reduce_scatter | solution.py:41
  (46 shorter events, 1.4 us)
Async XLA Ops:
  6.5 1.9 copy-start
  6.5 214.8 %all-gather.10.cloned.1.call-start = ((), (), s32[]{:S(2)}) async-start(), calls=%async_computation.2 | async-start | bytes 9437184 | tf_op jit(solution)/shard_map/all_gather | solution.py:26
  7.3 214.1 %all-gather.8.cloned.1.call-start = ((), (), s32[]{:S(2)}) async-start(), calls=%async_computation.1 | async-start | bytes 9437184 | tf_op jit(solution)/shard_map/all_gather | solution.py:21
  8.0 229.5 %all-gather.16.cloned.1.call-start = ((), (), s32[]{:S(2)}) async-start(), calls=%async_computation.5 | async-start | bytes 9437184 | tf_op jit(solution)/shard_map/all_gather | solution.py:26
  8.4 71.1 %collective-permute-start = (bf16[2,4096,192]{1,2,0:T(8,128)(2,1)S(1)}, bf16[2,4096,192]{1,2,0:T(8,128)(2,1)}, u32[]{:S(2)}, u32[]{:S(2)}) collective-permute-start(bf16[2,4096,192]{1,2,0:T(8,128)(2,1)S(1)} %copy-done), channel_id=1, source_target_pairs={{0,16},{16,0},{1,17},{17,1},{2,18},{18,2},{3,19},{19,3},{4,20},{20... | collective-permute-start | bytes 9437192 | tf_op jit(solution)/shard_map/ppermute | solution.py:20
  79.6 1.9 copy-start.1
  79.6 165.2 %all-gather.12.cloned.1.call-start = ((), (), s32[]{:S(2)}) async-start(), calls=%async_computation.3 | async-start | bytes 9437184 | tf_op jit(solution)/shard_map/all_gather | solution.py:27
  80.2 74.0 %copy-start.3 = (s32[128,8]{0,1:T(8,128)S(1)}, s32[128,8]{0,1:T(8,128)}, u32[]{:S(2)}) copy-start(s32[128,8]{0,1:T(8,128)} %param.8) | copy-start | bytes 12292
  80.2 74.0 %copy-start.4 = (s32[128,8]{0,1:T(8,128)S(1)}, s32[128,8]{0,1:T(8,128)}, u32[]{:S(2)}) copy-start(s32[128,8]{0,1:T(8,128)} %param.7) | copy-start | bytes 12292
  80.2 188.3 %all-gather.14.cloned.1.call-start = ((), (), s32[]{:S(2)}) async-start(), calls=%async_computation.4 | async-start | bytes 9437184 | tf_op jit(solution)/shard_map/all_gather | solution.py:28
  80.8 201.0 %all-gather.18.cloned.1.call-start = ((), (), s32[]{:S(2)}) async-start(), calls=%async_computation.6 | async-start | bytes 9437184 | tf_op jit(solution)/shard_map/all_gather | solution.py:27
  81.5 69.4 %collective-permute-start.1 = (bf16[2,4096,192]{1,2,0:T(8,128)(2,1)S(1)}, bf16[2,4096,192]{1,2,0:T(8,128)(2,1)}, u32[]{:S(2)}, u32[]{:S(2)}) collective-permute-start(bf16[2,4096,192]{1,2,0:T(8,128)(2,1)S(1)} %copy-done.1), channel_id=1, source_target_pairs={{0,16},{16,0},{1,17},{17,1},{2,18},{18,2},{3,19},{19,3},{4,20},{20... | collective-permute-start | bytes 9437192 | tf_op jit(solution)/shard_map/ppermute | solution.py:20
  150.9 1.9 copy-start.2
  150.9 147.0 %all-gather.20.cloned.1.call-start = ((), (), s32[]{:S(2)}) async-start(), calls=%async_computation.7 | async-start | bytes 9437184 | tf_op jit(solution)/shard_map/all_gather | solution.py:28
  152.8 68.5 %collective-permute-start.2 = (bf16[2,192,4096]{2,1,0:T(8,128)(2,1)S(1)}, bf16[2,192,4096]{2,1,0:T(8,128)(2,1)}, u32[]{:S(2)}, u32[]{:S(2)}) collective-permute-start(bf16[2,192,4096]{2,1,0:T(8,128)(2,1)S(1)} %copy-done.2), channel_id=1, source_target_pairs={{0,16},{16,0},{1,17},{17,1},{2,18},{18,2},{3,19},{19,3},{4,20},{20... | collective-permute-start | bytes 9437192 | tf_op jit(solution)/shard_map/ppermute | solution.py:20
  221.3 241.7 %reduce-scatter.2.cloned.1.call-start = ((), (), s32[]{:S(2)}) async-start(), calls=%async_computation.8 | async-start | bytes 9437184 | tf_op jit(solution)/shard_map/reduce_scatter | solution.py:41
  221.4 10.7 %copy-start.5 = (bf16[1024,4096]{1,0:T(8,128)(2,1)S(1)}, bf16[1024,4096]{1,0:T(8,128)(2,1)}, u32[]{:S(2)}) copy-start(bf16[1024,4096]{1,0:T(8,128)(2,1)} %all-gather.8.cloned.1.call-done) | copy-start | bytes 25165828
  221.4 11.5 %copy-start.6 = (bf16[2,4096,384]{1,2,0:T(8,128)(2,1)S(1)}, bf16[2,4096,384]{1,2,0:T(8,128)(2,1)}, u32[]{:S(2)}) copy-start(bf16[2,4096,384]{1,2,0:T(8,128)(2,1)} %all-gather.10.cloned.1.call-done) | copy-start | bytes 18874372
  244.8 9.5 %copy-start.7 = (bf16[2,4096,384]{1,2,0:T(8,128)(2,1)S(1)}, bf16[2,4096,384]{1,2,0:T(8,128)(2,1)}, u32[]{:S(2)}) copy-start(bf16[2,4096,384]{1,2,0:T(8,128)(2,1)} %all-gather.16.cloned.1.call-done) | copy-start | bytes 18874372
  254.3 7.2 %copy-start.8 = (bf16[2,4096,384]{1,2,0:T(8,128)(2,1)S(1)}, bf16[2,4096,384]{1,2,0:T(8,128)(2,1)}, u32[]{:S(2)}) copy-start(bf16[2,4096,384]{1,2,0:T(8,128)(2,1)} %all-gather.12.cloned.1.call-done) | copy-start | bytes 18874372
  254.3 7.2 %copy-start.11 = (f32[1024,384]{0,1:T(8,128)S(1)}, f32[1024,384]{0,1:T(8,128)}, u32[]{:S(2)}) copy-start(f32[1024,384]{0,1:T(8,128)} %fusion.5) | copy-start | bytes 4718596
  281.8 8.9 %copy-start.10 = (f32[1024,384]{0,1:T(8,128)S(1)}, f32[1024,384]{0,1:T(8,128)}, u32[]{:S(2)}) copy-start(f32[1024,384]{0,1:T(8,128)} %fusion.3) | copy-start | bytes 4718596
  281.8 8.9 %copy-start.9 = (bf16[2,4096,384]{1,2,0:T(8,128)(2,1)S(1)}, bf16[2,4096,384]{1,2,0:T(8,128)(2,1)}, u32[]{:S(2)}) copy-start(bf16[2,4096,384]{1,2,0:T(8,128)(2,1)} %all-gather.18.cloned.1.call-done) | copy-start | bytes 18874372
  290.8 7.1 %copy-start.12 = (bf16[1024,384]{0,1:T(8,128)(2,1)S(1)}, bf16[1024,384]{0,1:T(8,128)(2,1)}, u32[]{:S(2)}) copy-start(bf16[1024,384]{0,1:T(8,128)(2,1)} %multiply_convert_fusion) | copy-start | bytes 2359300
Sparse Core Ops, SparseCore 0:
  8.9 19.4 all-gather.9
  30.5 126.0 all-gather.7
  158.2 14.9 all-gather.15
  174.6 17.9 all-gather.11
  193.9 17.9 all-gather.13
  213.3 17.9 all-gather.17
  232.8 17.9 all-gather.19
  312.5 150.4 reduce-scatter.1

commit v4 on v3

--- a/solution.py
+++ b/solution.py
@@ -21,7 +21,7 @@
     all_tokens = lax.all_gather(tokens, "exp", axis=0, tiled=True)
     all_weight = lax.all_gather(weight, "exp", axis=0, tiled=True)
     mine = lax.dynamic_slice_in_dim(all_weight, lax.axis_index("exp") * local, local, axis=1)
-    total = None
+    pairs = []
     for w_gate, w_up, w_down in blocks:
         gate = lax.all_gather(w_gate, axes, axis=2, tiled=True)
         up = lax.all_gather(w_up, axes, axis=2, tiled=True)
@@ -32,15 +32,22 @@
             up_part = jnp.dot(all_tokens, up[one], preferred_element_type=jnp.float32)
             value = jax.nn.silu(gate_part) * up_part * mine[:, one : one + 1]
             hidden.append(value.astype(jnp.bfloat16))
-        term = jnp.dot(
-            jnp.concatenate(hidden, axis=1),
-            down.reshape(-1, down.shape[2]),
-            preferred_element_type=jnp.float32,
+        pairs.append((jnp.concatenate(hidden, axis=1), down.reshape(-1, down.shape[2])))
+    half = tokens.shape[1] // 2
+    outputs = []
+    for low in (0, half):
+        total = None
+        for hidden, down in pairs:
+            term = jnp.dot(
+                hidden, down[:, low : low + half], preferred_element_type=jnp.float32
+            )
+            total = term if total is None else total + term
+        outputs.append(
+            lax.psum_scatter(
+                total.astype(jnp.bfloat16), "exp", scatter_dimension=0, tiled=True
+            )
         )
-        total = term if total is None else total + term
-    return lax.psum_scatter(
-        total.astype(jnp.bfloat16), "exp", scatter_dimension=0, tiled=True
-    )
+    return jnp.concatenate(outputs, axis=1)
 
 
 def solution(mesh):

time: 470 us -> 495 us (1.053)
  waiting for transfers between devices: 325 us -> 343 us
    reduce_scatter x1 -> x2, waiting for transfers between devices: 151 us -> 168 us  [per_device(): lax.psum_scatter(total.astype(jnp.bfloat16), 'exp', scatter_dimension=0,...]
    dot_general x2 -> x4, matrix products: 27.8 us -> 30.5 us  [per_device(): jnp.dot(hidden, down[:, low:low + half], preferred_element_type=jnp.float32)]
  transfers between devices with their start and end apart: 11 -> 12, of which waited for: 4 -> 5; matrix products, arithmetic and copies ran while one was open for 16% -> 17% of each run, Pallas kernels for 0% -> 0%
where the time goes in v4:
time: 495 us
  waiting for transfers between devices  343 us (69%)
  matrix products  92.9 us (19%)
  blocking collectives  30.8 us (6%)
  between operations  13.4 us (3%)
  starting transfers between devices  6.68 us (1%)
  local copies, waits for them, and re-layouts  6.42 us (1%)
    ppermute x3, waiting for transfers between devices, per_device(): lax.ppermute(panel, 'x', swap)  172 us
    reduce_scatter x2, waiting for transfers between devices, per_device(): lax.psum_scatter(total.astype(jnp.bfloat16), 'exp', scatter_dimension=0,...  168 us
    dot_general x4, matrix products, per_device(): up_part = jnp.dot(all_tokens, up[one], preferred_element_type=jnp.float32)  34.4 us
    all_gather x1, blocking collectives, per_device(): all_weight = lax.all_gather(weight, 'exp', axis=0, tiled=True)  30.8 us
    dot_general x4, matrix products, per_device(): jnp.dot(hidden, down[:, low:low + half], preferred_element_type=jnp.float32)  30.5 us
    dot_general x4, matrix products, per_device(): jnp.dot(all_tokens, gate[one], preferred_element_type=jnp.float32)  28 us
  transfers between devices with their start and end apart: 12, of which 5 were waited for; matrix products, arithmetic and copies ran while one was open for 17% of the time, Pallas kernels for 0%

profile of v4, /device:TPU:0, one launch (start us, length us, event | category | flops | bytes accessed | tf_op | source)
XLA Modules:
  0.0 495.1 jit_solution(6120372469139042070)
XLA Ops:
  9.9 2.9 collective-permute-start
  12.8 68.2 %collective-permute-done = bf16[2,4096,192]{1,2,0:T(8,128)(2,1)} collective-permute-done((bf16[2,4096,192]{1,2,0:T(8,128)(2,1)S(1)}, bf16[2,4096,192]{1,2,0:T(8,128)(2,1)}, u32[]{:S(2)}, u32[]{:S(2)}) %collective-permute-start) | collective-permute-done | bytes 3145760 | tf_op jit(solution)/shard_map/ppermute | solution.py:20
  81.1 1.8 copy-done.1
  82.9 1.7 collective-permute-start.1
  84.7 67.6 %collective-permute-done.1 = bf16[2,4096,192]{1,2,0:T(8,128)(2,1)} collective-permute-done((bf16[2,4096,192]{1,2,0:T(8,128)(2,1)S(1)}, bf16[2,4096,192]{1,2,0:T(8,128)(2,1)}, u32[]{:S(2)}, u32[]{:S(2)}) %collective-permute-start.1) | collective-permute-done | bytes 3145760 | tf_op jit(solution)/shard_map/ppermute | solution.py:20
  152.4 1.8 copy-done.2
  155.7 30.8 %all_gather.27 = f32[1024,16]{0,1:T(8,128)S(1)} all-gather(f32[128,16]{0,1:T(8,128)S(1)} %select_reduce_fusion), channel_id=1, replica_groups=mesh['x'=2,'core'=2,'exp'=8] {'exp'}, dimensions={0}, use_global_device_ids=true | all-gather | bytes 73728 | tf_op jit(solution)/shard_map/all_gather | solution.py:22
  186.5 36.2 %collective-permute-done.2 = bf16[2,192,4096]{2,1,0:T(8,128)(2,1)} collective-permute-done((bf16[2,192,4096]{2,1,0:T(8,128)(2,1)S(1)}, bf16[2,192,4096]{2,1,0:T(8,128)(2,1)}, u32[]{:S(2)}, u32[]{:S(2)}) %collective-permute-start.2) | collective-permute-done | bytes 3145760 | tf_op jit(solution)/shard_map/ppermute | solution.py:20
  222.8 8.3 %fusion.11 = f32[1024,384]{0,1:T(8,128)S(1)} fusion(bf16[1024,4096]{1,0:T(8,128)(2,1)} %all-gather.8.cloned.1.call-done, bf16[2,4096,384]{1,2,0:T(8,128)(2,1)} %all-gather.10.cloned.1.call-done), kind=kOutput, calls=%fused_computation.19 | convolution fusion | flops 3221225472 | bytes 13107200 | tf_op jit(solution)/shard_map/dot_general | solution.py:31
  231.5 1.8 copy-done.6
  233.3 4.6 fusion.13
  237.9 10.1 %multiply_convert_fusion.3 = bf16[1024,384]{0,1:T(8,128)(2,1)S(1)} fusion(f32[1024,384]{0,1:T(8,128)} %fusion.13, bf16[1024,4096]{1,0:T(8,128)(2,1)} %all-gather.8.cloned.1.call-done, bf16[2,4096,384]{1,2,0:T(8,128)(2,1)} %all-gather.12.cloned.1.call-done, f32[1024]{0:T(1024)S(1)} %bitcast.44), kind=kOutput, calls=%fused_computation.29 | convolution fusion | flops 3223977984 | bytes 13897728 | tf_op jit(solution)/shard_map/dot_general | solution.py:32
  248.0 7.0 %multiply_convert_fusion.2 = bf16[1024,384]{0,1:T(8,128)(2,1)S(1)} fusion(f32[1024,384]{0,1:T(8,128)S(1)} %fusion.11, bf16[1024,4096]{1,0:T(8,128)(2,1)} %all-gather.8.cloned.1.call-done, bf16[2,4096,384]{1,2,0:T(8,128)(2,1)S(1)} %copy-done.7, f32[1024]{0:T(1024)S(1)} %bitcast.46), kind=kOutput, calls=%fused_computation.28 | convolution fusion | flops 3223977984 | bytes 13897728 | tf_op jit(solution)/shard_map/dot_general | solution.py:32
  255.1 7.7 %fusion.1 = f32[1024,2048]{1,0:T(8,128)} fusion(bf16[768,4096]{1,0:T(8,128)(2,1)} %bitcast.48, bf16[1024,384]{0,1:T(8,128)(2,1)S(1)} %multiply_convert_fusion.2, bf16[1024,384]{0,1:T(8,128)(2,1)S(1)} %multiply_convert_fusion.3), kind=kOutput, calls=%fused_computation.3 | convolution fusion | flops 3224371200 | bytes 13107200 | tf_op jit(solution)/shard_map/dot_general | solution.py:41
  262.8 9.0 %fusion.5 = f32[1024,384]{0,1:T(8,128)} fusion(bf16[1024,4096]{1,0:T(8,128)(2,1)} %all-gather.8.cloned.1.call-done, bf16[2,4096,384]{1,2,0:T(8,128)(2,1)} %all-gather.16.cloned.1.call-done), kind=kOutput, calls=%fused_computation.9 | convolution fusion | flops 3221225472 | bytes 13107200 | tf_op jit(solution)/shard_map/dot_general | solution.py:31
  271.8 6.1 %fusion.7 = f32[1024,384]{0,1:T(8,128)S(1)} fusion(bf16[1024,4096]{1,0:T(8,128)(2,1)} %all-gather.8.cloned.1.call-done, bf16[2,4096,384]{1,2,0:T(8,128)(2,1)S(1)} %copy-done.8), kind=kOutput, calls=%fused_computation.13 | convolution fusion | flops 3221225472 | bytes 13107200 | tf_op jit(solution)/shard_map/dot_general | solution.py:31
  278.0 9.3 %multiply_convert_fusion = bf16[1024,384]{0,1:T(8,128)(2,1)} fusion(f32[1024,384]{0,1:T(8,128)} %fusion.5, f32[1024]{0:T(1024)S(1)} %bitcast.47, bf16[1024,4096]{1,0:T(8,128)(2,1)} %all-gather.8.cloned.1.call-done, bf16[2,4096,384]{1,2,0:T(8,128)(2,1)} %all-gather.18.cloned.1.call-done), kind=kOutput, calls=%fused_computation.26 | convolution fusion | flops 3223977984 | bytes 13897728 | tf_op jit(solution)/shard_map/dot_general | solution.py:32
  287.3 7.9 %multiply_convert_fusion.1 = bf16[1024,384]{0,1:T(8,128)(2,1)} fusion(f32[1024,384]{0,1:T(8,128)S(1)} %fusion.7, f32[1024]{0:T(1024)S(1)} %bitcast.45, bf16[1024,4096]{1,0:T(8,128)(2,1)} %all-gather.8.cloned.1.call-done, bf16[2,4096,384]{1,2,0:T(8,128)(2,1)S(1)} %copy-done.9), kind=kOutput, calls=%fused_computation.27 | convolution fusion | flops 3223977984 | bytes 13897728 | tf_op jit(solution)/shard_map/dot_general | solution.py:32
  295.2 10.3 %add_convert_fusion = bf16[1024,2048]{1,0:T(8,128)(2,1)} fusion(f32[1024,2048]{1,0:T(8,128)} %fusion.1, bf16[768,4096]{1,0:T(8,128)(2,1)} %bitcast.50, bf16[1024,384]{0,1:T(8,128)(2,1)} %multiply_convert_fusion, bf16[1024,384]{0,1:T(8,128)(2,1)} %multiply_convert_fusion.1), kind=kOutput, calls=%fused_computation | convolution fusion | flops 3228565504 | bytes 17301504 | tf_op jit(solution)/shard_map/dot_general | solution.py:41
  305.9 5.5 %fusion.8 = f32[1024,2048]{1,0:T(8,128)S(1)} fusion(bf16[768,4096]{1,0:T(8,128)(2,1)} %bitcast.49, bf16[1024,384]{0,1:T(8,128)(2,1)S(1)} %multiply_convert_fusion.2, bf16[1024,384]{0,1:T(8,128)(2,1)S(1)} %multiply_convert_fusion.3), kind=kOutput, calls=%fused_computation.14 | convolution fusion | flops 3224371200 | bytes 13107200 | tf_op jit(solution)/shard_map/dot_general | solution.py:41
  311.4 7.0 %add_convert_fusion.1 = bf16[1024,2048]{1,0:T(8,128)(2,1)} fusion(f32[1024,2048]{1,0:T(8,128)S(1)} %fusion.8, bf16[768,4096]{1,0:T(8,128)(2,1)} %bitcast.51, bf16[1024,384]{0,1:T(8,128)(2,1)S(1)} %copy-done.10, bf16[1024,384]{0,1:T(8,128)(2,1)S(1)} %copy-done.11), kind=kOutput, calls=%fused_computation.1 | convolution fusion | flops 3228565504 | bytes 17301504 | tf_op jit(solution)/shard_map/dot_general | solution.py:41
  318.5 75.9 %reduce-scatter.5.cloned.1.call-done = bf16[128,2048]{1,0:T(8,128)(2,1)} async-done(((bf16[1024,2048]{1,0:T(8,128)(2,1)}), bf16[128,2048]{1,0:T(8,128)(2,1)}) %reduce-scatter.5.cloned.1.call-update) | async-done | bytes 524304 | tf_op jit(solution)/shard_map/reduce_scatter | solution.py:46
  394.4 91.9 %reduce-scatter.3.cloned.1.call-done = bf16[128,2048]{1,0:T(8,128)(2,1)} async-done(((bf16[1024,2048]{1,0:T(8,128)(2,1)}), bf16[128,2048]{1,0:T(8,128)(2,1)}) %reduce-scatter.3.cloned.1.call-update) | async-done | bytes 524304 | tf_op jit(solution)/shard_map/reduce_scatter | solution.py:46
  486.3 2.3 pad_maximum_fusion.2
  (50 shorter events, 5.8 us)
Async XLA Ops:
  6.5 216.2 %all-gather.10.cloned.1.call-start = ((), (), s32[]{:S(2)}) async-start(), calls=%async_computation.3 | async-start | bytes 9437184 | tf_op jit(solution)/shard_map/all_gather | solution.py:26
  7.3 215.5 %all-gather.8.cloned.1.call-start = ((), (), s32[]{:S(2)}) async-start(), calls=%async_computation.2 | async-start | bytes 9437184 | tf_op jit(solution)/shard_map/all_gather | solution.py:21
  8.0 1.9 copy-start
  8.0 229.9 %all-gather.12.cloned.1.call-start = ((), (), s32[]{:S(2)}) async-start(), calls=%async_computation.4 | async-start | bytes 9437184 | tf_op jit(solution)/shard_map/all_gather | solution.py:27
  8.8 246.3 %all-gather.14.cloned.1.call-start = ((), (), s32[]{:S(2)}) async-start(), calls=%async_computation.5 | async-start | bytes 9437184 | tf_op jit(solution)/shard_map/all_gather | solution.py:28
  9.3 253.5 %all-gather.16.cloned.1.call-start = ((), (), s32[]{:S(2)}) async-start(), calls=%async_computation.6 | async-start | bytes 9437184 | tf_op jit(solution)/shard_map/all_gather | solution.py:26
  9.9 71.1 %collective-permute-start = (bf16[2,4096,192]{1,2,0:T(8,128)(2,1)S(1)}, bf16[2,4096,192]{1,2,0:T(8,128)(2,1)}, u32[]{:S(2)}, u32[]{:S(2)}) collective-permute-start(bf16[2,4096,192]{1,2,0:T(8,128)(2,1)S(1)} %copy-done), channel_id=1, source_target_pairs={{0,16},{16,0},{1,17},{17,1},{2,18},{18,2},{3,19},{19,3},{4,20},{20... | collective-permute-start | bytes 9437192 | tf_op jit(solution)/shard_map/ppermute | solution.py:20
  81.0 1.9 copy-start.1
  81.0 74.6 %copy-start.3 = (s32[128,8]{0,1:T(8,128)S(1)}, s32[128,8]{0,1:T(8,128)}, u32[]{:S(2)}) copy-start(s32[128,8]{0,1:T(8,128)} %param.8) | copy-start | bytes 12292
  81.1 196.9 %all-gather.18.cloned.1.call-start = ((), (), s32[]{:S(2)}) async-start(), calls=%async_computation.7 | async-start | bytes 9437184 | tf_op jit(solution)/shard_map/all_gather | solution.py:27
  82.9 69.4 %collective-permute-start.1 = (bf16[2,4096,192]{1,2,0:T(8,128)(2,1)S(1)}, bf16[2,4096,192]{1,2,0:T(8,128)(2,1)}, u32[]{:S(2)}, u32[]{:S(2)}) collective-permute-start(bf16[2,4096,192]{1,2,0:T(8,128)(2,1)S(1)} %copy-done.1), channel_id=1, source_target_pairs={{0,16},{16,0},{1,17},{17,1},{2,18},{18,2},{3,19},{19,3},{4,20},{20... | collective-permute-start | bytes 9437192 | tf_op jit(solution)/shard_map/ppermute | solution.py:20
  152.3 1.9 copy-start.2
  152.3 3.3 copy-start.4
  152.4 142.9 %all-gather.20.cloned.1.call-start = ((), (), s32[]{:S(2)}) async-start(), calls=%async_computation.8 | async-start | bytes 9437184 | tf_op jit(solution)/shard_map/all_gather | solution.py:28
  154.2 68.5 %collective-permute-start.2 = (bf16[2,192,4096]{2,1,0:T(8,128)(2,1)S(1)}, bf16[2,192,4096]{2,1,0:T(8,128)(2,1)}, u32[]{:S(2)}, u32[]{:S(2)}) collective-permute-start(bf16[2,192,4096]{2,1,0:T(8,128)(2,1)S(1)} %copy-done.2), channel_id=1, source_target_pairs={{0,16},{16,0},{1,17},{17,1},{2,18},{18,2},{3,19},{19,3},{4,20},{20... | collective-permute-start | bytes 9437192 | tf_op jit(solution)/shard_map/ppermute | solution.py:20
  222.7 171.7 %reduce-scatter.5.cloned.1.call-start = ((), (), s32[]{:S(2)}) async-start(), calls=%async_computation.10 | async-start | bytes 4718592 | tf_op jit(solution)/shard_map/reduce_scatter | solution.py:46
  222.8 8.7 %copy-start.5 = (bf16[1024,4096]{1,0:T(8,128)(2,1)S(1)}, bf16[1024,4096]{1,0:T(8,128)(2,1)}, u32[]{:S(2)}) copy-start(bf16[1024,4096]{1,0:T(8,128)(2,1)} %all-gather.8.cloned.1.call-done) | copy-start | bytes 25165828
  222.8 10.5 %copy-start.6 = (bf16[2,4096,384]{1,2,0:T(8,128)(2,1)S(1)}, bf16[2,4096,384]{1,2,0:T(8,128)(2,1)}, u32[]{:S(2)}) copy-start(bf16[2,4096,384]{1,2,0:T(8,128)(2,1)} %all-gather.10.cloned.1.call-done) | copy-start | bytes 18874372
  237.9 10.1 %copy-start.7 = (bf16[2,4096,384]{1,2,0:T(8,128)(2,1)S(1)}, bf16[2,4096,384]{1,2,0:T(8,128)(2,1)}, u32[]{:S(2)}) copy-start(bf16[2,4096,384]{1,2,0:T(8,128)(2,1)} %all-gather.12.cloned.1.call-done) | copy-start | bytes 18874372
  262.8 9.0 %copy-start.8 = (bf16[2,4096,384]{1,2,0:T(8,128)(2,1)S(1)}, bf16[2,4096,384]{1,2,0:T(8,128)(2,1)}, u32[]{:S(2)}) copy-start(bf16[2,4096,384]{1,2,0:T(8,128)(2,1)} %all-gather.16.cloned.1.call-done) | copy-start | bytes 18874372
  277.9 9.4 %copy-start.9 = (bf16[2,4096,384]{1,2,0:T(8,128)(2,1)S(1)}, bf16[2,4096,384]{1,2,0:T(8,128)(2,1)}, u32[]{:S(2)}) copy-start(bf16[2,4096,384]{1,2,0:T(8,128)(2,1)} %all-gather.18.cloned.1.call-done) | copy-start | bytes 18874372
  305.5 5.9 %copy-start.10 = (bf16[1024,384]{0,1:T(8,128)(2,1)S(1)}, bf16[1024,384]{0,1:T(8,128)(2,1)}, u32[]{:S(2)}) copy-start(bf16[1024,384]{0,1:T(8,128)(2,1)} %multiply_convert_fusion) | copy-start | bytes 2359300
  305.5 5.9 %copy-start.11 = (bf16[1024,384]{0,1:T(8,128)(2,1)S(1)}, bf16[1024,384]{0,1:T(8,128)(2,1)}, u32[]{:S(2)}) copy-start(bf16[1024,384]{0,1:T(8,128)(2,1)} %multiply_convert_fusion.1) | copy-start | bytes 2359300
  305.6 180.8 %reduce-scatter.3.cloned.1.call-start = ((), (), s32[]{:S(2)}) async-start(), calls=%async_computation.9 | async-start | bytes 4718592 | tf_op jit(solution)/shard_map/reduce_scatter | solution.py:46
Sparse Core Ops, SparseCore 0:
  8.9 19.4 all-gather.9
  30.5 126.0 all-gather.7
  158.2 14.9 all-gather.11
  174.6 17.9 all-gather.13
  193.9 17.9 all-gather.15
  213.3 17.9 all-gather.17
  232.8 17.9 all-gather.19
  305.7 88.6 reduce-scatter.4
  398.5 87.7 reduce-scatter.2
